TPU v7x, 128 devices: a whole 4x4x4 slice. The times are simulated.
128 devices in a mesh: frame: 8 (over x_lo, z), row: 16 (over y, x_hi, core).
Axes of the slice: x: 4 (x_hi: 2, x_lo: 2; x = x_hi * 2 + x_lo), y: 4, z: 4, core: 2. Of those that a mesh axis runs over, the one named last changes fastest.
Arguments:
- tokens_a: bfloat16 [32, 2048, 1152], P('frame', 'row'), may hold values from -6 to 6
- modulate_a: float32 [3, 1152], replicated, may hold values from -3 to 3
- spatial_qkv: bfloat16 [1152, 3456], replicated, may hold values from -0.1875 to 0.1875
- spatial_proj: bfloat16 [1152, 1152], replicated, may hold values from -0.1875 to 0.1875
- spatial_gain: float32 [2, 72], replicated, may hold values from 1 to 10
- tokens_b: bfloat16 [32, 2048, 1152], P('frame', 'row'), may hold values from -6 to 6
- modulation_rows_b: float32 [3, 1152], replicated, may hold values from -3 to 3
- temporal_qkv: bfloat16 [1152, 3456], replicated, may hold values from -0.1875 to 0.1875
- temporal_proj: bfloat16 [1152, 1152], replicated, may hold values from -0.1875 to 0.1875
- temporal_gain: float32 [2, 72], replicated, may hold values from 1 to 10
Outputs:
- result_a: bfloat16 [32, 2048, 1152], P('frame', 'row')
- result_b: bfloat16 [32, 2048, 1152], P('frame', 'row')
All inputs are finite; a program needn't handle non-finite values.
Results may differ from a plain program's by a relative error of at most 0.012.
The roundings to bfloat16 on the way count: a program that leaves them out, or rounds other values in their place, can miss the bound.
Values may be sent and summed in bfloat16 or wider, within the bound.
A program may use at most 128 MiB of HBM per device.

v0:
```python
import functools
import math

import jax
import jax.numpy as jnp
from jax import lax
from jax.experimental import pallas as pl
from jax.experimental.pallas import tpu as pltpu
from jax.sharding import PartitionSpec as P

D = 1152
HEADS = 16
HD = 72
EXP_SCALE = math.log2(math.e) / math.sqrt(HD)
EPS = 1e-06
MESH = pl.DeviceIdType.MESH
F32 = jnp.float32
BF16 = jnp.bfloat16


def nt(a, b):
    return lax.dot_general(a, b, (((1,), (1,)), ((), ())), preferred_element_type=F32)


def nn(a, b):
    return lax.dot_general(a, b, (((1,), (0,)), ((), ())), preferred_element_type=F32)


def layer_norm(x, mod):
    center = x - jnp.mean(x, axis=-1, keepdims=True)
    spread = jnp.mean(center * center, axis=-1, keepdims=True)
    normed = center * lax.rsqrt(spread + EPS)
    return normed * (1.0 + mod[1:2, :]) + mod[0:1, :]


def head_norm(part, gain):
    p = part.reshape(part.shape[0] // HD, HD, part.shape[1])
    scale = lax.rsqrt(jnp.mean(p * p, axis=1, keepdims=True) + EPS)
    return p * scale * gain[None]


def gain_column(gain_row):
    rows = lax.broadcasted_iota(jnp.int32, (HD, HD), 0)
    cols = lax.broadcasted_iota(jnp.int32, (HD, HD), 1)
    return jnp.sum(jnp.where(rows == cols, gain_row, 0.0), axis=1, keepdims=True)


def with_ones(v):
    rows = lax.broadcasted_iota(jnp.int32, (8, v.shape[1]), 0)
    return jnp.concatenate([v, jnp.where(rows == 0, 1.0, 0.0)], axis=0).astype(BF16)


def kernel(
    ta, moda, wqa, wpa, ga, tb, modb, wqb, wpb, gb,
    ra, rb,
    ta_v, na, xa, xp, wa_raw, wt_tmp, wta, wb_raw, wtb, wpa_v, wpb_v,
    q_s, k_s, v_s, xb, nb, qb_s, kb_s, vb_s, mixb, rbs, mas, mx, ma_n, outa,
    sl, s_bt, r_bt, s_y, s_sib, s_x, r_x, r_xa, s_br, r_br, s_mx, r_mx,
):
    fi = lax.axis_index("frame")
    ri = lax.axis_index("row")
    y = ri // 4
    xh = (ri // 2) % 2
    c = ri % 2
    pair = y // 2
    my_f = 2 * pair + xh
    m = (y % 2) * 2 + c

    def row_dev(yy, hh, cc):
        return (fi, yy * 4 + hh * 2 + cc)

    sib = row_dev(y, xh, 1 - c)
    part_x = row_dev(y, 1 - xh, c)
    mate_y = 2 * pair + 1 - (y % 2)
    mate = row_dev(mate_y, xh, c)
    other_y = [2 * (1 - pair) + (y % 2), 2 * (1 - pair) + 1 - (y % 2)]
    others = [row_dev(yy, xh, c) for yy in other_y]
    r_part = y * 4 + (1 - xh) * 2 + c

    def remote(src, dst, ss, rs, dev):
        return pltpu.make_async_remote_copy(
            src_ref=src, dst_ref=dst, send_sem=ss, recv_sem=rs, device_id=dev, device_id_type=MESH
        )

    loads = {}

    def load(name, src, dst, k):
        loads[name] = pltpu.make_async_copy(src, dst, sl.at[k])
        loads[name].start()

    load("ta", ta, ta_v, 0)
    for part in range(3):
        start = pl.multiple_of(part * D + 256 * m, 128)
        load(("wa", part), wqa.at[:, pl.ds(start, 384)], wa_raw.at[part], 1 + part)
    load("wb", wqb, wb_raw, 4)
    load("wpa", wpa, wpa_v, 5)
    load("wpb", wpb, wpb_v, 6)
    load("tb", tb.at[:, pl.ds(pl.multiple_of(16 * fi, 16), 16), :], xb.at[fi], 7)

    barrier = pltpu.get_barrier_semaphore()
    for k in range(1, 16):
        pl.semaphore_signal(barrier, inc=1, device_id=(fi, (ri + k) % 16), device_id_type=MESH)
    for k in range(1, 8):
        pl.semaphore_signal(barrier, inc=1, device_id=((fi + k) % 8, ri), device_id_type=MESH)
    pl.semaphore_wait(barrier, 22)

    sends = []
    for k in range(1, 8):
        g = (fi + k) % 8
        cp = remote(
            tb.at[:, pl.ds(pl.multiple_of(16 * g, 16), 16), :],
            xb.at[fi], s_bt.at[k], r_bt.at[fi], (g, ri),
        )
        cp.start()
        sends.append(cp)

    loads["ta"].wait()

    def norm_frame(f, dst):
        dst[...] = layer_norm(ta_v[f].astype(F32), moda).astype(BF16)

    def start(src, dst, ss, rs, dev):
        cp = remote(src, dst, ss, rs, dev)
        cp.start()
        sends.append(cp)

    norm_frame(2 * (1 - pair) + xh, na.at[0])
    for k in range(2):
        start(na.at[0], xa.at[ri], s_y.at[k], r_xa.at[ri], others[k])
    norm_frame(2 * (1 - pair) + 1 - xh, na.at[1])
    start(na.at[1], xp, s_x.at[0], r_x, part_x)
    norm_frame(my_f, xa.at[ri])
    start(xa.at[ri], xa.at[ri], s_y.at[2], r_xa.at[ri], mate)
    start(xa.at[ri], xa.at[ri], s_sib.at[0], r_xa.at[ri], sib)
    norm_frame(2 * pair + 1 - xh, na.at[2])
    start(na.at[2], xa.at[ri], s_x.at[1], r_xa.at[ri], part_x)

    for part in range(3):
        loads[("wa", part)].wait()
        wt_tmp[...] = wa_raw[part].T
        wta[part * 288:(part + 1) * 288, :] = wt_tmp[pl.ds(pl.multiple_of(32 * m, 32), 288), :]
    loads["wb"].wait()

    @pl.loop(0, 27)
    def _(i):
        at = pl.multiple_of(i * 128, 128)
        wtb[pl.ds(at, 128), :] = wb_raw[:, pl.ds(at, 128)].T

    gain_a = [gain_column(ga[0:1, :]), gain_column(ga[1:2, :])]
    gain_b = [gain_column(gb[0:1, :]), gain_column(gb[1:2, :])]

    def arrived(yy, hh, cc, frm):
        r = yy * 4 + hh * 2 + cc
        remote(xa.at[r], xa.at[r], s_sib.at[0], r_xa.at[r], frm).wait_recv()

    def pass_on(k, yy, hh):
        r = yy * 4 + hh * 2 + c
        start(xa.at[r], xa.at[r], s_sib.at[k], r_xa.at[r], sib)

    arrived(mate_y, xh, c, mate)
    pass_on(1, mate_y, xh)
    for k in range(2):
        arrived(other_y[k], xh, c, others[k])
        pass_on(2 + k, other_y[k], xh)

    def norm_b(g):
        x = layer_norm(xb[g].astype(F32).reshape(64, D), modb).reshape(4, 2, 8, D)
        for half in range(2):
            nb[half, pl.ds(pl.multiple_of(g * 32, 32), 32), :] = (
                x[:, half].reshape(32, D).astype(BF16)
            )

    loads["tb"].wait()
    norm_b(fi)
    for k in range(1, 8):
        g = (fi + 8 - k) % 8
        remote(xb.at[g], xb.at[g], s_bt.at[0], r_bt.at[g], (g, ri)).wait_recv()
        norm_b(g)

    def qkv_b(half):
        x = nb[half]
        cols = slice(half * 256, half * 256 + 256)
        q = head_norm(nt(wtb[0:D, :], x), gain_b[0])
        for h in range(HEADS):
            qb_s[h, cols, :] = q[h].T.astype(BF16)
        kk = head_norm(nt(wtb[D:2 * D, :], x), gain_b[1])
        for h in range(HEADS):
            kb_s[h, :, cols] = kk[h].astype(BF16)
        v = nt(wtb[2 * D:3 * D, :], x)
        for h in range(HEADS):
            vb_s[h, :, cols] = with_ones(v[h * HD:(h + 1) * HD])

    qkv_b(0)
    remote(xp, xp, s_x.at[0], r_x, part_x).wait_recv()
    for k in range(2):
        start(xp, xa.at[r_part], s_y.at[3 + k], r_xa.at[r_part], others[k])
    qkv_b(1)
    arrived(y, 1 - xh, c, part_x)
    start(xa.at[r_part], xa.at[r_part], s_y.at[5], r_xa.at[r_part], mate)
    pass_on(4, y, 1 - xh)

    same = (
        lax.broadcasted_iota(jnp.int32, (256, 256), 0) % 8
        == lax.broadcasted_iota(jnp.int32, (256, 256), 1) % 8
    )

    @pl.loop(0, HEADS // 2)
    def _(hp):
        for half in range(2):
            cols = slice(half * 256, half * 256 + 256)
            outs = []
            for j in range(2):
                h = hp * 2 + j
                s = jnp.where(same, nn(qb_s[h, cols, :], kb_s[h, :, cols]), -1e30)
                top = jnp.max(s, axis=1, keepdims=True)
                p = jnp.exp2((s - top) * EXP_SCALE).astype(BF16)
                ot = nt(vb_s[h, :, cols], p)
                outs.append(ot[:HD] * (1.0 / ot[HD:HD + 1]))
            mixb[pl.ds(pl.multiple_of(hp * 144, 144), 144), cols] = (
                jnp.concatenate(outs, axis=0).astype(BF16)
            )

    arrived(mate_y, 1 - xh, c, mate)
    pass_on(5, mate_y, 1 - xh)

    loads["wpb"].wait()
    halves = []
    for half in range(2):
        proj = nn(mixb[:, half * 256:half * 256 + 256].T, wpb_v[...])
        halves.append((proj * modb[2:3, :]).reshape(32, 8, D))
    delta = jnp.concatenate([h[:, None] for h in halves], axis=1).reshape(8, 4, 16, D)
    rbs[...] = (xb[...].astype(F32) + delta).astype(BF16)

    for k in range(2):
        arrived(other_y[k], 1 - xh, c, others[k])
        pass_on(6 + k, other_y[k], 1 - xh)

    at_fi = pl.ds(pl.multiple_of(16 * fi, 16), 16)
    for k in range(1, 8):
        g = (fi + k) % 8
        start(rbs.at[g], rb.at[:, at_fi, :], s_br.at[k], r_br.at[fi], (g, ri))
    own_b = pltpu.make_async_copy(rbs.at[fi], rb.at[:, at_fi, :], s_br.at[0])
    own_b.start()

    def qkv_a(yy, hh):
        g = yy * 2 + hh
        x = xa[pl.ds(2 * g, 2)].reshape(256, D)
        rows = pl.ds(pl.multiple_of(g * 256, 256), 256)
        out = nt(wta[...], x)
        q = head_norm(out[0:288], gain_a[0])
        kk = head_norm(out[288:576], gain_a[1])
        for h in range(4):
            q_s[h, rows, :] = q[h].T.astype(BF16)
            k_s[h, :, rows] = kk[h].astype(BF16)
            v_s[h, :, rows] = with_ones(out[576 + h * HD:576 + (h + 1) * HD])

    for hh in (xh, 1 - xh):
        for yy in (y, mate_y, other_y[0], other_y[1]):
            arrived(yy, hh, 1 - c, sib)
            qkv_a(yy, hh)

    def scores(h, blk):
        return nn(q_s[h, pl.ds(pl.multiple_of(blk * 256, 256), 256), :], k_s[h])

    @pl.loop(0, 4)
    def _(i):
        b0 = 2 * ((i + my_f) % 4)
        items = [(b, h) for b in range(2) for h in range(4)]
        s = scores(items[0][1], b0)
        outs = []
        for n, (b, h) in enumerate(items):
            following = None
            if n + 1 < len(items):
                following = scores(items[n + 1][1], b0 + items[n + 1][0])
            top = jnp.max(s, axis=1, keepdims=True)
            p = jnp.exp2((s - top) * EXP_SCALE).astype(BF16)
            ot = nt(v_s[h], p)
            outs.append(ot[:HD] * (1.0 / ot[HD:HD + 1]))
            if h == 3:
                block = jnp.concatenate(outs, axis=0).astype(BF16)
                outs = []
                for cc in range(2):
                    r = (b0 + b) * 2 + cc
                    mas[r] = block[:, cc * 128:(cc + 1) * 128]
            s = following
        for k in range(4):
            r = b0 * 2 + k

            @pl.when(r != ri)
            def _():
                remote(
                    mas.at[r], mx.at[my_f, pl.ds(pl.multiple_of(288 * m, 32), 288), :],
                    s_mx.at[r], r_mx.at[my_f * 4 + m], (fi, r),
                ).start()

    own_m = pltpu.make_async_copy(
        mas.at[ri], mx.at[my_f, pl.ds(pl.multiple_of(288 * m, 32), 288), :], s_mx.at[ri]
    )
    own_m.start()
    own_m.wait()

    loads["wpa"].wait()
    for k in range(1, 16):
        r = (ri + k) % 16
        f_r = 2 * (r // 8) + (r // 2) % 2
        m_r = ((r // 4) % 2) * 2 + r % 2
        slot = mx.at[f_r, pl.ds(pl.multiple_of(288 * m_r, 32), 288), :]
        remote(slot, slot, s_mx.at[r], r_mx.at[f_r * 4 + m_r], (fi, r)).wait_recv()
    for f in range(4):
        ma_n[f * 128:(f + 1) * 128, :] = mx[f].T
    proj = nn(ma_n[...], wpa_v[...]).reshape(4, 128, D)
    outa[...] = (ta_v[...].astype(F32) + moda[2:3, :] * proj).astype(BF16)
    out_copy = pltpu.make_async_copy(outa, ra, sl.at[0])
    out_copy.start()

    for k in range(1, 8):
        g = (fi + k) % 8
        at_g = pl.ds(pl.multiple_of(16 * g, 16), 16)
        remote(rbs.at[g], rb.at[:, at_g, :], s_br.at[0], r_br.at[g], (g, ri)).wait_recv()
    for cp in sends:
        cp.wait_send()
    for k in range(1, 16):
        r = (ri + k) % 16
        remote(mas.at[r], mas.at[r], s_mx.at[r], r_mx.at[0], (fi, r)).wait_send()
    own_b.wait()
    out_copy.wait()


def per_device(*args):
    any_spec = pl.BlockSpec(memory_space=pl.ANY)
    vmem = pl.BlockSpec(memory_space=pltpu.VMEM)
    v = pltpu.VMEM
    dma = pltpu.SemaphoreType.DMA
    shape = jax.ShapeDtypeStruct((4, 128, D), BF16)
    specs = [any_spec, vmem, any_spec, any_spec, vmem]
    return pl.pallas_call(
        kernel,
        out_shape=(shape, shape),
        in_specs=specs + specs,
        out_specs=(any_spec, any_spec),
        scratch_shapes=[
            v((4, 128, D), BF16),
            v((3, 128, D), BF16),
            v((16, 128, D), BF16),
            v((128, D), BF16),
            v((3, D, 384), BF16),
            v((384, D), BF16),
            v((864, D), BF16),
            v((D, 3 * D), BF16),
            v((3 * D, D), BF16),
            v((D, D), BF16),
            v((D, D), BF16),
            v((4, 2048, HD), BF16),
            v((4, HD, 2048), BF16),
            v((4, 80, 2048), BF16),
            v((8, 4, 16, D), BF16),
            v((2, 256, D), BF16),
            v((HEADS, 512, HD), BF16),
            v((HEADS, HD, 512), BF16),
            v((HEADS, 80, 512), BF16),
            v((D, 512), BF16),
            v((8, 4, 16, D), BF16),
            v((16, 288, 128), BF16),
            v((4, D, 128), BF16),
            v((512, D), BF16),
            v((4, 128, D), BF16),
            dma((8,)),
            dma((8,)),
            dma((8,)),
            dma((6,)),
            dma((8,)),
            dma((2,)),
            dma,
            dma((16,)),
            dma((8,)),
            dma((8,)),
            dma((16,)),
            dma((16,)),
        ],
        compiler_params=pltpu.CompilerParams(
            collective_id=0, has_side_effects=True, vmem_limit_bytes=63 << 20
        ),
        cost_estimate=pl.CostEstimate(
            flops=25_000_000_000, bytes_accessed=40_000_000, transcendentals=20_000_000
        ),
    )(*args)


def solution(mesh):
    tokens = P("frame", "row", None)
    return jax.shard_map(
        per_device,
        mesh=mesh,
        in_specs=(tokens, P(), P(), P(), P(), tokens, P(), P(), P(), P()),
        out_specs=(tokens, tokens),
        check_vma=False,
    )
```

profile of v0, /device:TPU:121, one launch (start us, length us, event | category | flops | bytes accessed | tf_op | source)
XLA Modules:
  0.0 95.9 jit_solution(14455138905675268079)
XLA Ops:
  0.6 91.8 %shard_map.113 = (bf16[4,128,1152]{2,1,0:T(8,128)(2,1)}, bf16[4,128,1152]{2,1,0:T(8,128)(2,1)}) custom-call(bf16[4,128,1152]{2,1,0:T(8,128)(2,1)} %ta.1, f32[3,1152]{1,0:T(4,128)} %moda.1, bf16[1152,3456]{1,0:T(8,128)(2,1)} %wqa.1, bf16[1152,1152]{1,0:T(8,128)(2,1)} %wpa.1, f32[2,72]{1,0:T(2,128)} %ga.1, bf16[4,128,1152]{2,1,0:T(8,128)(2,1)} %tb.1, ...), custom_call_target="tpu_custom_call" | custom-call | flops 24999999488 | bytes 40000000 | tf_op jit(solution)/shard_map/pallas_call | solution.py:336
  92.4 0.0 copy-start
  92.4 2.5 %copy.14 = bf16[4,128,1152]{2,1,0:T(8,128)(2,1)} copy(bf16[4,128,1152]{2,1,0:T(8,128)(2,1)} %get-tuple-element.4) | data formatting | bytes 2359296
  94.9 0.0 copy-done
  94.9 1.0 %copy.15 = bf16[4,128,1152]{2,1,0:T(8,128)(2,1)} copy(bf16[4,128,1152]{2,1,0:T(8,128)(2,1)S(1)} %copy-done) | data formatting | bytes 2359296
Async XLA Ops:
  92.4 2.5 %copy-start = (bf16[4,128,1152]{2,1,0:T(8,128)(2,1)S(1)}, bf16[4,128,1152]{2,1,0:T(8,128)(2,1)}, u32[]{:S(2)}) copy-start(bf16[4,128,1152]{2,1,0:T(8,128)(2,1)} %get-tuple-element.5) | copy-start | bytes 3538948
where the time goes:
time: 96.1 us; the launch traced here: 95.9 us
  Pallas kernels  91.8 us (96%)
  local copies, waits for them, and re-layouts  3.49 us (4%)
    pallas_call x1, Pallas kernels, per_device(): pl.pallas_call(kernel, out_shape=(shape, shape), in_specs=specs + specs,...  91.8 us
    unnamed x4, local copies, waits for them, and re-layouts  3.49 us

commit v1 on v0

v1 whole, which is shorter than its diff:
```python
import functools
import math

import jax
import jax.numpy as jnp
from jax import lax
from jax.experimental import pallas as pl
from jax.experimental.pallas import tpu as pltpu
from jax.sharding import PartitionSpec as P

D = 1152
HEADS = 16
HD = 72
EXP_SCALE = math.log2(math.e) / math.sqrt(HD)
EPS = 1e-06
MESH = pl.DeviceIdType.MESH
F32 = jnp.float32
BF16 = jnp.bfloat16


def nt(a, b):
    return lax.dot_general(a, b, (((1,), (1,)), ((), ())), preferred_element_type=F32)


def nn(a, b):
    return lax.dot_general(a, b, (((1,), (0,)), ((), ())), preferred_element_type=F32)


def layer_norm(x, mod):
    center = x - jnp.mean(x, axis=-1, keepdims=True)
    spread = jnp.mean(center * center, axis=-1, keepdims=True)
    normed = center * lax.rsqrt(spread + EPS)
    return normed * (1.0 + mod[1:2, :]) + mod[0:1, :]


def head_norm(part, gain):
    p = part.reshape(part.shape[0] // HD, HD, part.shape[1])
    scale = lax.rsqrt(jnp.mean(p * p, axis=1, keepdims=True) + EPS)
    return p * scale * gain[None]


def gain_column(gain_row):
    rows = lax.broadcasted_iota(jnp.int32, (HD, HD), 0)
    cols = lax.broadcasted_iota(jnp.int32, (HD, HD), 1)
    return jnp.sum(jnp.where(rows == cols, gain_row, 0.0), axis=1, keepdims=True)


def with_ones(v):
    rows = lax.broadcasted_iota(jnp.int32, (8, v.shape[1]), 0)
    return jnp.concatenate([v, jnp.where(rows == 0, 1.0, 0.0)], axis=0).astype(BF16)


def kernel(
    ta, moda, wqa, wpa, ga, tb, modb, wqb, wpb, gb,
    ra, rb,
    ta_v, tb_v, na, xa, wa_raw, wt_tmp, wta, wb_raw, wtb, wpa_v, wpb_v,
    q_s, k_s, v_s, xb, nb, qb_s, kb_s, vb_s, mixb, rbs, mas, mx, ma_n,
    sl, s_bt, r_bt, s_d, s_mate, s_sib, r_xa, s_br, r_br, s_mx, r_mx,
):
    fi = lax.axis_index("frame")
    ri = lax.axis_index("row")
    y = ri // 4
    xh = (ri // 2) % 2
    c = ri % 2
    pair = y // 2
    my_f = 2 * pair + xh
    m = (y % 2) * 2 + c

    def row_dev(yy, hh, cc):
        return (fi, yy * 4 + hh * 2 + cc)

    sib = row_dev(y, xh, 1 - c)
    mate_y = 2 * pair + 1 - (y % 2)
    mate = row_dev(mate_y, xh, c)
    across_y = 3 - y
    mate_across_y = 3 - mate_y

    def remote(src, dst, ss, rs, dev):
        return pltpu.make_async_remote_copy(
            src_ref=src, dst_ref=dst, send_sem=ss, recv_sem=rs, device_id=dev, device_id_type=MESH
        )

    loads = {}

    def load(name, src, dst, k):
        loads[name] = pltpu.make_async_copy(src, dst, sl.at[k])
        loads[name].start()

    load("tb", tb, tb_v, 7)
    load("ta", ta, ta_v, 0)
    for part in range(3):
        first = pl.multiple_of(part * D + 256 * m, 128)
        load(("wa", part), wqa.at[:, pl.ds(first, 384)], wa_raw.at[part], 1 + part)
    load("wb", wqb, wb_raw, 4)
    load("wpa", wpa, wpa_v, 5)
    load("wpb", wpb, wpb_v, 6)

    barrier = pltpu.get_barrier_semaphore()
    near = [sib, mate, row_dev(across_y, xh, c), row_dev(y, 1 - xh, c), row_dev(across_y, 1 - xh, c)]
    near += [((fi + k) % 8, ri) for k in range(1, 8)]
    for device in near:
        pl.semaphore_signal(barrier, inc=1, device_id=device, device_id_type=MESH)
    pl.semaphore_wait(barrier, len(near))

    sends = []
    loads["tb"].wait()
    for k in range(1, 8):
        g = (fi + k) % 8
        cp = remote(
            tb_v.at[:, pl.ds(pl.multiple_of(16 * g, 16), 16), :],
            xb.at[fi], s_bt.at[k], r_bt.at[fi], (g, ri),
        )
        cp.start()
        sends.append(cp)

    loads["ta"].wait()

    def norm_frame(f, dst):
        dst[...] = layer_norm(ta_v[f].astype(F32), moda).astype(BF16)

    def start(src, dst, ss, rs, dev):
        cp = remote(src, dst, ss, rs, dev)
        cp.start()
        sends.append(cp)

    norm_frame(2 * (1 - pair) + xh, na.at[0])
    start(na.at[0], xa.at[ri], s_d.at[0], r_xa.at[ri, 0], row_dev(across_y, xh, c))
    norm_frame(my_f, xa.at[ri])
    start(xa.at[ri], xa.at[ri], s_mate.at[0, 0], r_xa.at[ri, 0], mate)
    start(xa.at[ri], xa.at[ri], s_sib.at[0, 0], r_xa.at[ri, 0], sib)
    norm_frame(2 * (1 - pair) + 1 - xh, na.at[1])
    norm_frame(2 * pair + 1 - xh, na.at[2])

    whole = ((0, 128),)
    in_halves = ((0, 64), (64, 64))

    def piece(r, k, part):
        return xa.at[r, pl.ds(*part), :], r_xa.at[r, k]

    def arrived(yy, hh, cc, frm, parts=whole):
        r = yy * 4 + hh * 2 + cc
        for k, part in enumerate(parts):
            ref, sem = piece(r, k, part)
            remote(ref, ref, s_sib.at[0, 0], sem, frm).wait_recv()

    def pass_on(yy, hh, frm, targets, parts=whole):
        r = yy * 4 + hh * 2 + c
        for k, part in enumerate(parts):
            ref, sem = piece(r, k, part)
            remote(ref, ref, s_sib.at[0, 0], sem, frm).wait_recv()
            for send_sem, device in targets:
                start(ref, ref, send_sem.at[k], sem, device)

    def from_source(n, yy, hh, parts=whole):
        targets = ((s_mate.at[n], mate), (s_sib.at[n], sib))
        pass_on(yy, hh, row_dev(yy, hh, c), targets, parts)

    def from_mate(n, yy, hh, parts=whole):
        pass_on(yy, hh, mate, ((s_sib.at[n], sib),), parts)

    for part in range(3):
        loads[("wa", part)].wait()
        wt_tmp[...] = wa_raw[part].T
        wta[part * 288:(part + 1) * 288, :] = wt_tmp[pl.ds(pl.multiple_of(32 * m, 32), 288), :]
    from_source(1, across_y, xh)
    from_mate(4, mate_y, xh)
    loads["wb"].wait()

    @pl.loop(0, 27)
    def _(i):
        at = pl.multiple_of(i * 128, 128)
        wtb[pl.ds(at, 128), :] = wb_raw[:, pl.ds(at, 128)].T

    gain_a = [gain_column(ga[0:1, :]), gain_column(ga[1:2, :])]
    gain_b = [gain_column(gb[0:1, :]), gain_column(gb[1:2, :])]

    def qkv_a(yy, hh):
        g = yy * 2 + hh
        x = xa[pl.ds(2 * g, 2)].reshape(256, D)
        rows = pl.ds(pl.multiple_of(g * 256, 256), 256)
        out = nt(wta[...], x)
        q = head_norm(out[0:288], gain_a[0])
        kk = head_norm(out[288:576], gain_a[1])
        for h in range(4):
            q_s[h, rows, :] = q[h].T.astype(BF16)
            k_s[h, :, rows] = kk[h].astype(BF16)
            v_s[h, :, rows] = with_ones(out[576 + h * HD:576 + (h + 1) * HD])

    def group_a(yy, hh, parts=whole):
        arrived(yy, hh, 1 - c, sib, parts)
        qkv_a(yy, hh)

    group_a(y, xh)
    group_a(mate_y, xh)
    group_a(across_y, xh)

    def norm_b(g):
        x = layer_norm(xb[g].astype(F32).reshape(64, D), modb).reshape(4, 2, 8, D)
        for half in range(2):
            nb[half, pl.ds(pl.multiple_of(g * 32, 32), 32), :] = (
                x[:, half].reshape(32, D).astype(BF16)
            )

    xb[fi] = tb_v[:, pl.ds(pl.multiple_of(16 * fi, 16), 16), :]
    norm_b(fi)
    for k in range(1, 8):
        g = (fi + 8 - k) % 8
        remote(xb.at[g], xb.at[g], s_bt.at[0], r_bt.at[g], (g, ri)).wait_recv()
        norm_b(g)

    def qkv_b(half):
        x = nb[half]
        cols = slice(half * 256, half * 256 + 256)
        q = head_norm(nt(wtb[0:D, :], x), gain_b[0])
        for h in range(HEADS):
            qb_s[h, cols, :] = q[h].T.astype(BF16)
        kk = head_norm(nt(wtb[D:2 * D, :], x), gain_b[1])
        for h in range(HEADS):
            kb_s[h, :, cols] = kk[h].astype(BF16)
        v = nt(wtb[2 * D:3 * D, :], x)
        for h in range(HEADS):
            vb_s[h, :, cols] = with_ones(v[h * HD:(h + 1) * HD])

    start(na.at[1], xa.at[ri], s_d.at[1], r_xa.at[ri, 0], row_dev(across_y, 1 - xh, c))
    from_mate(5, mate_across_y, xh)
    qkv_b(0)
    qkv_b(1)
    for k, part in enumerate(in_halves):
        start(
            na.at[2, pl.ds(*part), :], xa.at[ri, pl.ds(*part), :], s_d.at[2 + k], r_xa.at[ri, k],
            row_dev(y, 1 - xh, c),
        )

    same = (
        lax.broadcasted_iota(jnp.int32, (256, 256), 0) % 8
        == lax.broadcasted_iota(jnp.int32, (256, 256), 1) % 8
    )

    def attend_b(hp):
        blocks = [(j, half) for j in range(2) for half in range(2)]
        cols = [slice(0, 256), slice(256, 512)]
        ss = [
            jnp.where(same, nn(qb_s[hp * 2 + j, cols[half], :], kb_s[hp * 2 + j, :, cols[half]]), -1e30)
            for j, half in blocks
        ]
        tops = [jnp.max(s, axis=1, keepdims=True) for s in ss]
        ps = [jnp.exp2((s - top) * EXP_SCALE).astype(BF16) for s, top in zip(ss, tops)]
        ots = [nt(vb_s[hp * 2 + j, :, cols[half]], p) for (j, half), p in zip(blocks, ps)]
        ots = [ot[:HD] * (1.0 / ot[HD:HD + 1]) for ot in ots]
        for half in range(2):
            mixb[pl.ds(pl.multiple_of(hp * 144, 144), 144), cols[half]] = (
                jnp.concatenate([ots[half], ots[2 + half]], axis=0).astype(BF16)
            )

    pl.loop(0, 4)(attend_b)
    from_source(2, across_y, 1 - xh)
    pl.loop(4, 8)(attend_b)
    loads["wpb"].wait()
    halves = []
    for half in range(2):
        proj = nn(mixb[:, half * 256:half * 256 + 256].T, wpb_v[...])
        halves.append((proj * modb[2:3, :]).reshape(32, 8, D))
    delta = jnp.concatenate([h[:, None] for h in halves], axis=1).reshape(8, 4, 16, D)
    rbs[...] = (xb[...].astype(F32) + delta).astype(BF16)

    group_a(mate_across_y, xh)
    from_source(3, y, 1 - xh, in_halves)
    at_fi = pl.ds(pl.multiple_of(16 * fi, 16), 16)
    for k in range(1, 8):
        g = (fi + k) % 8
        start(rbs.at[g], rb.at[:, at_fi, :], s_br.at[k], r_br.at[fi], (g, ri))
    own_b = pltpu.make_async_copy(rbs.at[fi], rb.at[:, at_fi, :], s_br.at[0])
    own_b.start()

    from_mate(6, mate_across_y, 1 - xh)
    group_a(across_y, 1 - xh)
    group_a(mate_across_y, 1 - xh)
    group_a(y, 1 - xh, in_halves)
    from_mate(7, mate_y, 1 - xh, in_halves)
    group_a(mate_y, 1 - xh, in_halves)

    def scores(h, blk):
        return nn(q_s[h, pl.ds(pl.multiple_of(blk * 256, 256), 256), :], k_s[h])

    my_slot = mx.at[my_f, pl.ds(pl.multiple_of(288 * m, 32), 288), :]

    def send_mixed(r):
        @pl.when(r != ri)
        def _():
            remote(mas.at[r], my_slot, s_mx.at[r], r_mx.at[my_f * 4 + m], (fi, r)).start()

    @pl.loop(0, 4)
    def _(i):
        b0 = 2 * ((i + my_f) % 4)
        items = [(b, h) for b in range(2) for h in range(4)]
        s = scores(items[0][1], b0)
        outs = []
        for n, (b, h) in enumerate(items):
            following = None
            if n + 1 < len(items):
                following = scores(items[n + 1][1], b0 + items[n + 1][0])
            top = jnp.max(s, axis=1, keepdims=True)
            p = jnp.exp2((s - top) * EXP_SCALE).astype(BF16)
            ot = nt(v_s[h], p)
            outs.append(ot[:HD] * (1.0 / ot[HD:HD + 1]))
            if h == 3:
                block = jnp.concatenate(outs, axis=0).astype(BF16)
                outs = []
                for cc in range(2):
                    r = (b0 + b) * 2 + cc
                    mas[r] = block[:, cc * 128:(cc + 1) * 128]
                for cc in range(2):
                    send_mixed((b0 + b) * 2 + cc)
            s = following

    own_m = pltpu.make_async_copy(mas.at[ri], my_slot, s_mx.at[ri])
    own_m.start()
    own_m.wait()

    loads["wpa"].wait()

    def project(frames):
        for n, f in enumerate(frames):
            for mm in range(4):
                r = (2 * (f // 2) + mm // 2) * 4 + (f % 2) * 2 + mm % 2

                @pl.when(r != ri)
                def _():
                    slot = mx.at[f, mm * 288:(mm + 1) * 288, :]
                    remote(slot, slot, s_mx.at[r], r_mx.at[f * 4 + mm], (fi, r)).wait_recv()
            ma_n[n * 128:(n + 1) * 128, :] = mx[f].T
        proj = nn(ma_n[:len(frames) * 128, :], wpa_v[...])
        for n, f in enumerate(frames):
            delta = moda[2:3, :] * proj[n * 128:(n + 1) * 128]
            ra[f] = (ta_v[f].astype(F32) + delta).astype(BF16)

    order = [(ri // 4 + 4 - n) % 4 for n in range(4)]
    project(order[:3])
    project(order[3:])

    for k in range(1, 8):
        g = (fi + k) % 8
        at_g = pl.ds(pl.multiple_of(16 * g, 16), 16)
        remote(rbs.at[g], rb.at[:, at_g, :], s_br.at[0], r_br.at[g], (g, ri)).wait_recv()
    for cp in sends:
        cp.wait_send()
    for k in range(1, 16):
        r = (ri + k) % 16
        remote(mas.at[r], mas.at[r], s_mx.at[r], r_mx.at[0], (fi, r)).wait_send()
    own_b.wait()


def per_device(*args):
    any_spec = pl.BlockSpec(memory_space=pl.ANY)
    vmem = pl.BlockSpec(memory_space=pltpu.VMEM)
    v = pltpu.VMEM
    dma = pltpu.SemaphoreType.DMA
    specs = [any_spec, vmem, any_spec, any_spec, vmem]
    return pl.pallas_call(
        kernel,
        out_shape=(v((4, 128, D), BF16), v((4, 128, D), BF16)),
        in_specs=specs + specs,
        out_specs=(vmem, vmem),
        scratch_shapes=[
            v((4, 128, D), BF16),
            v((4, 128, D), BF16),
            v((3, 128, D), BF16),
            v((16, 128, D), BF16),
            v((3, D, 384), BF16),
            v((384, D), BF16),
            v((864, D), BF16),
            v((D, 3 * D), BF16),
            v((3 * D, D), BF16),
            v((D, D), BF16),
            v((D, D), BF16),
            v((4, 2048, HD), BF16),
            v((4, HD, 2048), BF16),
            v((4, 80, 2048), BF16),
            v((8, 4, 16, D), BF16),
            v((2, 256, D), BF16),
            v((HEADS, 512, HD), BF16),
            v((HEADS, HD, 512), BF16),
            v((HEADS, 80, 512), BF16),
            v((D, 512), BF16),
            v((8, 4, 16, D), BF16),
            v((16, 288, 128), BF16),
            v((4, D, 128), BF16),
            v((512, D), BF16),
            dma((8,)),
            dma((8,)),
            dma((8,)),
            dma((4,)),
            dma((4, 2)),
            dma((8, 2)),
            dma((16, 2)),
            dma((8,)),
            dma((8,)),
            dma((16,)),
            dma((16,)),
        ],
        compiler_params=pltpu.CompilerParams(
            collective_id=0, has_side_effects=True, vmem_limit_bytes=60 << 20
        ),
        cost_estimate=pl.CostEstimate(
            flops=25_000_000_000, bytes_accessed=40_000_000, transcendentals=20_000_000
        ),
    )(*args)


def solution(mesh):
    tokens = P("frame", "row", None)
    return jax.shard_map(
        per_device,
        mesh=mesh,
        in_specs=(tokens, P(), P(), P(), P(), tokens, P(), P(), P(), P()),
        out_specs=(tokens, tokens),
        check_vma=False,
    )
```

time: 96.1 us -> 85.9 us (0.89)
  the two profiles are of different devices: /device:TPU:121 before, /device:TPU:13 now
where the time goes in v1:
time: 85.9 us; the launch traced here: 85.7 us
  Pallas kernels  83 us (97%)
  local copies, waits for them, and re-layouts  2.03 us (2%)
    pallas_call x1, Pallas kernels, per_device(): pl.pallas_call(kernel, out_shape=(v((4, 128, D), BF16), v((4, 128, D), BF...  83 us
    unnamed x2, local copies, waits for them, and re-layouts  2.03 us

profile of v1, /device:TPU:13, one launch (start us, length us, event | category | flops | bytes accessed | tf_op | source)
XLA Modules:
  0.0 85.7 jit_solution(3277934579471592597)
XLA Ops:
  0.6 83.0 %shard_map.113 = (bf16[4,128,1152]{2,1,0:T(8,128)(2,1)S(1)}, bf16[4,128,1152]{2,1,0:T(8,128)(2,1)S(1)}) custom-call(bf16[4,128,1152]{2,1,0:T(8,128)(2,1)} %ta.1, f32[3,1152]{1,0:T(4,128)} %moda.1, bf16[1152,3456]{1,0:T(8,128)(2,1)} %wqa.1, bf16[1152,1152]{1,0:T(8,128)(2,1)} %wpa.1, f32[2,72]{1,0:T(2,128)} %ga.1, bf16[4,128,1152]{2,1,0:T(8,128)(2,1)} %tb.1, ...), custom_call_target="tpu_custom_call" | custom-call | flops 24999999488 | bytes 40000000 | tf_op jit(solution)/shard_map/pallas_call | solution.py:359
  83.7 1.0 %copy.14 = bf16[4,128,1152]{2,1,0:T(8,128)(2,1)} copy(bf16[4,128,1152]{2,1,0:T(8,128)(2,1)S(1)} %get-tuple-element.2) | data formatting | bytes 2359296
  84.7 1.0 %copy.15 = bf16[4,128,1152]{2,1,0:T(8,128)(2,1)} copy(bf16[4,128,1152]{2,1,0:T(8,128)(2,1)S(1)} %get-tuple-element.3) | data formatting | bytes 2359296

commit v2 on v1

--- a/solution.py
+++ b/solution.py
@@ -54,8 +54,8 @@
     ta, moda, wqa, wpa, ga, tb, modb, wqb, wpb, gb,
     ra, rb,
     ta_v, tb_v, na, xa, wa_raw, wt_tmp, wta, wb_raw, wtb, wpa_v, wpb_v,
-    q_s, k_s, v_s, xb, nb, qb_s, kb_s, vb_s, mixb, rbs, mas, mx, ma_n,
-    sl, s_bt, r_bt, s_d, s_mate, s_sib, r_xa, s_br, r_br, s_mx, r_mx,
+    q_s, k_s, v_s, part_out, tops, xb, nb, qb_s, kb_s, vb_s, mixb, rbs, mas, mx, ma_n,
+    sl, s_wb, s_bt, r_bt, s_d, s_mate, s_sib, r_xa, s_br, r_br, s_mx, r_mx,
 ):
     fi = lax.axis_index("frame")
     ri = lax.axis_index("row")
@@ -88,12 +88,6 @@
 
     load("tb", tb, tb_v, 7)
     load("ta", ta, ta_v, 0)
-    for part in range(3):
-        first = pl.multiple_of(part * D + 256 * m, 128)
-        load(("wa", part), wqa.at[:, pl.ds(first, 384)], wa_raw.at[part], 1 + part)
-    load("wb", wqb, wb_raw, 4)
-    load("wpa", wpa, wpa_v, 5)
-    load("wpb", wpb, wpb_v, 6)
 
     barrier = pltpu.get_barrier_semaphore()
     near = [sib, mate, row_dev(across_y, xh, c), row_dev(y, 1 - xh, c), row_dev(across_y, 1 - xh, c)]
@@ -129,6 +123,18 @@
     start(xa.at[ri], xa.at[ri], s_mate.at[0, 0], r_xa.at[ri, 0], mate)
     start(xa.at[ri], xa.at[ri], s_sib.at[0, 0], r_xa.at[ri, 0], sib)
     norm_frame(2 * (1 - pair) + 1 - xh, na.at[1])
+    for part in range(3):
+        first = pl.multiple_of(part * D + 256 * m, 128)
+        load(("wa", part), wqa.at[:, pl.ds(first, 384)], wa_raw.at[part], 1 + part)
+    def load_b(k, slot):
+        return pltpu.make_async_copy(
+            wqb.at[:, pl.ds(pl.multiple_of(k * 384, 128), 384)], wb_raw.at[slot], s_wb.at[slot]
+        )
+
+    for k in range(3):
+        load_b(k, k).start()
+    load("wpa", wpa, wpa_v, 5)
+    load("wpb", wpb, wpb_v, 6)
     norm_frame(2 * pair + 1 - xh, na.at[2])
 
     whole = ((0, 128),)
@@ -143,20 +149,20 @@
             ref, sem = piece(r, k, part)
             remote(ref, ref, s_sib.at[0, 0], sem, frm).wait_recv()
 
-    def pass_on(yy, hh, frm, targets, parts=whole):
+    def pass_on(yy, hh, frm, targets, parts=whole, first=0):
         r = yy * 4 + hh * 2 + c
-        for k, part in enumerate(parts):
+        for k, part in enumerate(parts, first):
             ref, sem = piece(r, k, part)
             remote(ref, ref, s_sib.at[0, 0], sem, frm).wait_recv()
             for send_sem, device in targets:
                 start(ref, ref, send_sem.at[k], sem, device)
 
-    def from_source(n, yy, hh, parts=whole):
+    def from_source(n, yy, hh, parts=whole, first=0):
         targets = ((s_mate.at[n], mate), (s_sib.at[n], sib))
-        pass_on(yy, hh, row_dev(yy, hh, c), targets, parts)
-
-    def from_mate(n, yy, hh, parts=whole):
-        pass_on(yy, hh, mate, ((s_sib.at[n], sib),), parts)
+        pass_on(yy, hh, row_dev(yy, hh, c), targets, parts, first)
+
+    def from_mate(n, yy, hh, parts=whole, first=0):
+        pass_on(yy, hh, mate, ((s_sib.at[n], sib),), parts, first)
 
     for part in range(3):
         loads[("wa", part)].wait()
@@ -164,18 +170,25 @@
         wta[part * 288:(part + 1) * 288, :] = wt_tmp[pl.ds(pl.multiple_of(32 * m, 32), 288), :]
     from_source(1, across_y, xh)
     from_mate(4, mate_y, xh)
-    loads["wb"].wait()
-
-    @pl.loop(0, 27)
-    def _(i):
-        at = pl.multiple_of(i * 128, 128)
-        wtb[pl.ds(at, 128), :] = wb_raw[:, pl.ds(at, 128)].T
+
+    @pl.loop(0, 9)
+    def _(k):
+        slot = k % 3
+        load_b(k, slot).wait()
+        for tile in range(3):
+            at = pl.multiple_of(k * 384 + tile * 128, 128)
+            wtb[pl.ds(at, 128), :] = wb_raw[slot, :, tile * 128:(tile + 1) * 128].T
+
+        @pl.when(k < 6)
+        def _():
+            load_b(k + 3, slot).start()
 
     gain_a = [gain_column(ga[0:1, :]), gain_column(ga[1:2, :])]
     gain_b = [gain_column(gb[0:1, :]), gain_column(gb[1:2, :])]
 
     def qkv_a(yy, hh):
         g = yy * 2 + hh
+        cols = pl.ds(pl.multiple_of((0 if hh is xh else 1024) + yy * 256, 256), 256)
         x = xa[pl.ds(2 * g, 2)].reshape(256, D)
         rows = pl.ds(pl.multiple_of(g * 256, 256), 256)
         out = nt(wta[...], x)
@@ -183,8 +196,8 @@
         kk = head_norm(out[288:576], gain_a[1])
         for h in range(4):
             q_s[h, rows, :] = q[h].T.astype(BF16)
-            k_s[h, :, rows] = kk[h].astype(BF16)
-            v_s[h, :, rows] = with_ones(out[576 + h * HD:576 + (h + 1) * HD])
+            k_s[h, :, cols] = kk[h].astype(BF16)
+            v_s[h, :, cols] = with_ones(out[576 + h * HD:576 + (h + 1) * HD])
 
     def group_a(yy, hh, parts=whole):
         arrived(yy, hh, 1 - c, sib, parts)
@@ -207,6 +220,13 @@
         g = (fi + 8 - k) % 8
         remote(xb.at[g], xb.at[g], s_bt.at[0], r_bt.at[g], (g, ri)).wait_recv()
         norm_b(g)
+
+    def send_half(k):
+        part = in_halves[k]
+        start(
+            na.at[2, pl.ds(*part), :], xa.at[ri, pl.ds(*part), :], s_d.at[2 + k], r_xa.at[ri, k],
+            row_dev(y, 1 - xh, c),
+        )
 
     def qkv_b(half):
         x = nb[half]
@@ -225,11 +245,7 @@
     from_mate(5, mate_across_y, xh)
     qkv_b(0)
     qkv_b(1)
-    for k, part in enumerate(in_halves):
-        start(
-            na.at[2, pl.ds(*part), :], xa.at[ri, pl.ds(*part), :], s_d.at[2 + k], r_xa.at[ri, k],
-            row_dev(y, 1 - xh, c),
-        )
+    send_half(0)
 
     same = (
         lax.broadcasted_iota(jnp.int32, (256, 256), 0) % 8
@@ -253,8 +269,10 @@
             )
 
     pl.loop(0, 4)(attend_b)
+    send_half(1)
     from_source(2, across_y, 1 - xh)
     pl.loop(4, 8)(attend_b)
+
     loads["wpb"].wait()
     halves = []
     for half in range(2):
@@ -264,6 +282,24 @@
     rbs[...] = (xb[...].astype(F32) + delta).astype(BF16)
 
     group_a(mate_across_y, xh)
+    from_mate(6, mate_across_y, 1 - xh)
+
+    def first_part(yy):
+        rows = pl.ds(pl.multiple_of((yy * 2 + xh) * 256, 256), 256)
+
+        def near_scores(h):
+            return nn(q_s[h, rows, :], k_s[h, :, :1024])
+
+        s = near_scores(0)
+        for h in range(4):
+            following = near_scores(h + 1) if h < 3 else None
+            top = jnp.max(s, axis=1, keepdims=True)
+            tops[yy, h] = top
+            p = jnp.exp2((s - top) * EXP_SCALE).astype(BF16)
+            part_out[yy, h] = nt(v_s[h, :, :1024], p)
+            s = following
+
+    pl.loop(0, 1)(first_part)
     from_source(3, y, 1 - xh, in_halves)
     at_fi = pl.ds(pl.multiple_of(16 * fi, 16), 16)
     for k in range(1, 8):
@@ -271,16 +307,14 @@
         start(rbs.at[g], rb.at[:, at_fi, :], s_br.at[k], r_br.at[fi], (g, ri))
     own_b = pltpu.make_async_copy(rbs.at[fi], rb.at[:, at_fi, :], s_br.at[0])
     own_b.start()
-
-    from_mate(6, mate_across_y, 1 - xh)
     group_a(across_y, 1 - xh)
+    pl.loop(1, 3)(first_part)
+    from_mate(7, mate_y, 1 - xh, in_halves[:1], 0)
+    pl.loop(3, 4)(first_part)
     group_a(mate_across_y, 1 - xh)
+    from_mate(7, mate_y, 1 - xh, in_halves[1:], 1)
     group_a(y, 1 - xh, in_halves)
-    from_mate(7, mate_y, 1 - xh, in_halves)
     group_a(mate_y, 1 - xh, in_halves)
-
-    def scores(h, blk):
-        return nn(q_s[h, pl.ds(pl.multiple_of(blk * 256, 256), 256), :], k_s[h])
 
     my_slot = mx.at[my_f, pl.ds(pl.multiple_of(288 * m, 32), 288), :]
 
@@ -291,26 +325,36 @@
 
     @pl.loop(0, 4)
     def _(i):
-        b0 = 2 * ((i + my_f) % 4)
+        yy = (i + my_f) % 4
+        blocks = [yy * 2 + 1 - xh, yy * 2 + xh]
         items = [(b, h) for b in range(2) for h in range(4)]
-        s = scores(items[0][1], b0)
+
+        def scores(b, h):
+            q = q_s[h, pl.ds(pl.multiple_of(blocks[b] * 256, 256), 256), :]
+            return nn(q, k_s[h, :, 1024:] if b == 1 else k_s[h])
+
+        s = scores(*items[0])
         outs = []
         for n, (b, h) in enumerate(items):
-            following = None
-            if n + 1 < len(items):
-                following = scores(items[n + 1][1], b0 + items[n + 1][0])
+            following = scores(*items[n + 1]) if n + 1 < len(items) else None
             top = jnp.max(s, axis=1, keepdims=True)
+            if b == 1:
+                before = tops[yy, h]
+                top = jnp.maximum(top, before)
+                shrink = jnp.broadcast_to(jnp.exp2((before - top) * EXP_SCALE), (256, 128)).T[0:1]
             p = jnp.exp2((s - top) * EXP_SCALE).astype(BF16)
-            ot = nt(v_s[h], p)
+            if b == 1:
+                ot = nt(v_s[h, :, 1024:], p) + part_out[yy, h] * shrink
+            else:
+                ot = nt(v_s[h], p)
             outs.append(ot[:HD] * (1.0 / ot[HD:HD + 1]))
             if h == 3:
                 block = jnp.concatenate(outs, axis=0).astype(BF16)
                 outs = []
                 for cc in range(2):
-                    r = (b0 + b) * 2 + cc
-                    mas[r] = block[:, cc * 128:(cc + 1) * 128]
+                    mas[blocks[b] * 2 + cc] = block[:, cc * 128:(cc + 1) * 128]
                 for cc in range(2):
-                    send_mixed((b0 + b) * 2 + cc)
+                    send_mixed(blocks[b] * 2 + cc)
             s = following
 
     own_m = pltpu.make_async_copy(mas.at[ri], my_slot, s_mx.at[ri])
@@ -369,13 +413,15 @@
             v((3, D, 384), BF16),
             v((384, D), BF16),
             v((864, D), BF16),
-            v((D, 3 * D), BF16),
+            v((3, D, 384), BF16),
             v((3 * D, D), BF16),
             v((D, D), BF16),
             v((D, D), BF16),
             v((4, 2048, HD), BF16),
             v((4, HD, 2048), BF16),
             v((4, 80, 2048), BF16),
+            v((4, 4, 80, 256), F32),
+            v((4, 4, 256, 1), F32),
             v((8, 4, 16, D), BF16),
             v((2, 256, D), BF16),
             v((HEADS, 512, HD), BF16),
@@ -387,6 +433,7 @@
             v((4, D, 128), BF16),
             v((512, D), BF16),
             dma((8,)),
+            dma((3,)),
             dma((8,)),
             dma((8,)),
             dma((4,)),

time: 85.9 us -> 85.5 us (level)
  no operation moved by 1% of the time
where the time goes in v2:
time: 85.5 us; the launch traced here: 85.2 us
  Pallas kernels  82.5 us (96%)
  local copies, waits for them, and re-layouts  2.03 us (2%)
    pallas_call x1, Pallas kernels, per_device(): pl.pallas_call(kernel, out_shape=(v((4, 128, D), BF16), v((4, 128, D), BF...  82.5 us
    unnamed x2, local copies, waits for them, and re-layouts  2.03 us

profile of v2, /device:TPU:13, one launch (start us, length us, event | category | flops | bytes accessed | tf_op | source)
XLA Modules:
  0.0 85.2 jit_solution(1523302350698184295)
XLA Ops:
  0.6 82.5 %shard_map.113 = (bf16[4,128,1152]{2,1,0:T(8,128)(2,1)S(1)}, bf16[4,128,1152]{2,1,0:T(8,128)(2,1)S(1)}) custom-call(bf16[4,128,1152]{2,1,0:T(8,128)(2,1)} %ta.1, f32[3,1152]{1,0:T(4,128)} %moda.1, bf16[1152,3456]{1,0:T(8,128)(2,1)} %wqa.1, bf16[1152,1152]{1,0:T(8,128)(2,1)} %wpa.1, f32[2,72]{1,0:T(2,128)} %ga.1, bf16[4,128,1152]{2,1,0:T(8,128)(2,1)} %tb.1, ...), custom_call_target="tpu_custom_call" | custom-call | flops 24999999488 | bytes 40000000 | tf_op jit(solution)/shard_map/pallas_call | solution.py:403
  83.1 1.0 %copy.14 = bf16[4,128,1152]{2,1,0:T(8,128)(2,1)} copy(bf16[4,128,1152]{2,1,0:T(8,128)(2,1)S(1)} %get-tuple-element.2) | data formatting | bytes 2359296
  84.2 1.0 %copy.15 = bf16[4,128,1152]{2,1,0:T(8,128)(2,1)} copy(bf16[4,128,1152]{2,1,0:T(8,128)(2,1)S(1)} %get-tuple-element.3) | data formatting | bytes 2359296
